TPU v7x, 128 devices: a whole 4x4x4 slice. The times are simulated.
128 devices in a mesh: row: 16 (over x, y_lo, core), col: 8 (over y_hi, z).
Axes of the slice: x: 4, y: 4 (y_hi: 2, y_lo: 2; y = y_hi * 2 + y_lo), z: 4, core: 2. Of those that a mesh axis runs over, the one named last changes fastest.
Arguments:
- blocks: bfloat16 [1024, 64, 128, 128], P('row', 'col'), may hold values from -0.109375 to 0.109375
- columns: int32 [1024, 64], P('row', 'col'), may hold values from 0 to 127
- counts: int32 [1024, 8], P('row', 'col'), may hold values from 1 to 8, as said below
- vectors: bfloat16 [1024, 32, 128], P(('col', 'row')), may hold values from -6 to 6
Outputs:
- first_image: bfloat16 [1024, 32, 128], P(('row', 'col'))
- first_back: bfloat16 [1024, 32, 128], P(('col', 'row'))
- second_image: bfloat16 [1024, 32, 128], P(('row', 'col'))
- second_back: bfloat16 [1024, 32, 128], P(('col', 'row'))
Inputs may be any that keep to these rules, and one draw needn't show every extreme that they name: `counts`: the live slots are the leading ones; the largest count, 8, is reached in every draw.
All inputs are finite; a program needn't handle non-finite values.
Results may differ from a plain program's by a relative error of at most 0.022.
Values may be sent and summed in bfloat16 or wider, within the bound.
A program may use at most 64 MiB of HBM per device.

v0:
```python
import jax
import jax.numpy as jnp
from jax import lax
from jax.sharding import PartitionSpec as P


def pick_blocks(column_vecs, columns, active):
    return column_vecs[columns] * active.astype(jnp.bfloat16)[:, :, None, None]


def forward_terms(blocks, picked):
    return jnp.einsum("isrc,iskc->ikr", blocks, picked, preferred_element_type=jnp.float32)


def adjoint_terms(blocks, columns, active, row_vecs, col_count):
    terms = jnp.einsum("isrc,ikr->iskc", blocks, row_vecs, preferred_element_type=jnp.float32)
    terms = terms * active.astype(jnp.float32)[:, :, None, None]
    slot_total = terms.shape[0] * terms.shape[1]
    return jax.ops.segment_sum(
        terms.reshape(slot_total, terms.shape[2], terms.shape[3]),
        columns.reshape(slot_total),
        num_segments=col_count,
    )


def body(blocks, columns, counts, vectors):
    vec_count = vectors.shape[0]
    col_count = vec_count * lax.axis_size("row")
    slot_ids = jnp.arange(columns.shape[1], dtype=jnp.int32)
    active = slot_ids[None, :] < counts
    results = []
    current = vectors
    for round_no in range(2):
        column_vecs = lax.all_gather(current, "row", axis=0, tiled=True)
        picked = pick_blocks(column_vecs, columns, active)
        forward_out = lax.psum_scatter(
            forward_terms(blocks, picked), "col", scatter_dimension=0, tiled=True
        ).astype(jnp.bfloat16)
        row_vecs = lax.all_gather(forward_out, "col", axis=0, tiled=True)
        partial_value = adjoint_terms(blocks, columns, active, row_vecs, col_count)
        adjoint_out = lax.psum_scatter(
            partial_value.astype(jnp.bfloat16), "row", scatter_dimension=0, tiled=True
        )
        results.append(forward_out)
        results.append(adjoint_out)
        current = adjoint_out
    return (results[0], results[1], results[2], results[3])


def solution(mesh):
    in_specs = (
        P("row", "col", None, None),
        P("row", "col"),
        P("row", "col"),
        P(("col", "row"), None, None),
    )
    out_specs = (
        P(("row", "col"), None, None),
        P(("col", "row"), None, None),
        P(("row", "col"), None, None),
        P(("col", "row"), None, None),
    )
    return jax.shard_map(body, mesh=mesh, in_specs=in_specs, out_specs=out_specs, check_vma=False)
```

profile of v0, /device:TPU:0, one launch (start us, length us, event | category | flops | bytes accessed | tf_op | source)
XLA Modules:
  0.0 566.4 jit_solution(17264336816287896016)
XLA Ops:
  7.2 0.7 all-gather.3.cloned.1.call-update
  7.9 0.7 compare_select_fusion
  8.8 0.7 fusion.14
  9.6 35.0 %all-gather.3.cloned.1.call-done = bf16[128,32,128]{2,1,0:T(8,128)(2,1)} async-done(((bf16[8,32,128]{2,1,0:T(8,128)(2,1)}), bf16[128,32,128]{2,1,0:T(8,128)(2,1)}) %all-gather.3.cloned.1.call-update) | async-done | bytes 1048592 | tf_op jit(solution)/shard_map/all_gather | solution.py:34
  44.6 4.4 gather_fusion
  49.0 10.9 %fusion.6 = f32[64,32,128]{2,1,0:T(8,128)} fusion(bf16[64,8,128,128]{3,2,1,0:T(8,128)(2,1)} %param.4, bf16[64,8,32,128]{3,2,1,0:T(8,128)(2,1)} %bitcast.32, bf16[64,8]{1,0:T(8,128)(2,1)S(1)} %get-tuple-element.5), kind=kOutput, calls=%fused_computation.12 | convolution fusion | flops 538968064 | bytes 22021120 | tf_op jit(solution)/shard_map/isrc,iskc->ikr/dot_general | solution.py:12
  60.1 71.8 %reduce-scatter.5.cloned.1.call-done = f32[8,32,128]{2,1,0:T(8,128)} async-done(((f32[64,32,128]{2,1,0:T(8,128)}), f32[8,32,128]{2,1,0:T(8,128)}) %reduce-scatter.5.cloned.1.call-update) | async-done | bytes 131088 | tf_op jit(solution)/shard_map/reduce_scatter | solution.py:36
  131.9 0.9 convert_element_type.29
  132.9 34.9 %all_gather.13 = bf16[64,32,128]{2,1,0:T(8,128)(2,1)S(1)} all-gather(bf16[8,32,128]{2,1,0:T(8,128)(2,1)S(1)} %convert_element_type.29), channel_id=1, replica_groups=mesh['row'=16,'col'=8] {'col'}, dimensions={0}, use_global_device_ids=true | all-gather | bytes 589824 | tf_op jit(solution)/shard_map/all_gather | solution.py:39
  167.8 11.3 %broadcast_multiply_fusion.1 = f32[64,32,8,128]{3,1,2,0:T(8,128)} fusion(f32[64,8]{1,0:T(8,128)S(1)} %get-tuple-element.4, bf16[64,8,128,128]{3,2,1,0:T(8,128)(2,1)} %param.4, bf16[64,32,128]{2,1,0:T(8,128)(2,1)S(1)} %all_gather.13), kind=kOutput, calls=%fused_computation.7 | convolution fusion | flops 538968064 | bytes 25692160 | tf_op jit(solution)/shard_map/isrc,ikr->iskc/dot_general | solution.py:16
  179.1 0.2 broadcast.40.clone
  179.4 44.6 %scatter_fusion = f32[128,32,128]{2,1,0:T(8,128)S(1)} fusion(f32[128,32,128]{2,1,0:T(8,128)S(1)} %broadcast.40.clone, s32[512]{0:T(512)S(1)} %reshape.78, f32[512,32,128]{2,1,0:T(8,128)} %bitcast.30), kind=kCustom, calls=%fused_computation.2 | custom fusion | flops 2097152 | bytes 25167872 | tf_op jit(solution)/shard_map/scatter-add | solution.py:19
  223.9 1.2 convert_element_type.31
  225.2 60.3 %reduce-scatter.7.cloned.1.call-done = bf16[8,32,128]{2,1,0:T(8,128)(2,1)} async-done(((bf16[128,32,128]{2,1,0:T(8,128)(2,1)}), bf16[8,32,128]{2,1,0:T(8,128)(2,1)}) %reduce-scatter.7.cloned.1.call-update) | async-done | bytes 65552 | tf_op jit(solution)/shard_map/reduce_scatter | solution.py:41
  285.5 33.0 %all-gather.5.cloned.1.call-done = bf16[128,32,128]{2,1,0:T(8,128)(2,1)} async-done(((bf16[8,32,128]{2,1,0:T(8,128)(2,1)}), bf16[128,32,128]{2,1,0:T(8,128)(2,1)}) %all-gather.5.cloned.1.call-update) | async-done | bytes 1048592 | tf_op jit(solution)/shard_map/all_gather | solution.py:34
  318.5 4.4 gather_fusion.1
  322.9 10.9 %fusion.9 = f32[64,32,128]{2,1,0:T(8,128)} fusion(bf16[64,8,128,128]{3,2,1,0:T(8,128)(2,1)} %param.4, bf16[64,8,32,128]{3,2,1,0:T(8,128)(2,1)} %bitcast.31, bf16[64,8]{1,0:T(8,128)(2,1)S(1)} %get-tuple-element.5), kind=kOutput, calls=%fused_computation.13 | convolution fusion | flops 538968064 | bytes 22021120 | tf_op jit(solution)/shard_map/isrc,iskc->ikr/dot_general | solution.py:12
  333.9 72.1 %reduce-scatter.9.cloned.1.call-done = f32[8,32,128]{2,1,0:T(8,128)} async-done(((f32[64,32,128]{2,1,0:T(8,128)}), f32[8,32,128]{2,1,0:T(8,128)}) %reduce-scatter.9.cloned.1.call-update) | async-done | bytes 131088 | tf_op jit(solution)/shard_map/reduce_scatter | solution.py:36
  405.9 0.9 convert_element_type.32
  406.9 35.1 %all_gather.15 = bf16[64,32,128]{2,1,0:T(8,128)(2,1)S(1)} all-gather(bf16[8,32,128]{2,1,0:T(8,128)(2,1)S(1)} %convert_element_type.32), channel_id=1, replica_groups=mesh['row'=16,'col'=8] {'col'}, dimensions={0}, use_global_device_ids=true | all-gather | bytes 589824 | tf_op jit(solution)/shard_map/all_gather | solution.py:39
  441.9 11.3 %broadcast_multiply_fusion = f32[64,32,8,128]{3,1,2,0:T(8,128)} fusion(f32[64,8]{1,0:T(8,128)S(1)} %get-tuple-element.4, bf16[64,8,128,128]{3,2,1,0:T(8,128)(2,1)} %param.4, bf16[64,32,128]{2,1,0:T(8,128)(2,1)S(1)} %all_gather.15), kind=kOutput, calls=%fused_computation.6 | convolution fusion | flops 538968064 | bytes 25692160 | tf_op jit(solution)/shard_map/isrc,ikr->iskc/dot_general | solution.py:16
  453.5 44.6 %scatter_fusion.1 = f32[128,32,128]{2,1,0:T(8,128)S(1)} fusion(f32[128,32,128]{2,1,0:T(8,128)S(1)} %broadcast.40, s32[512]{0:T(512)S(1)} %reshape.78, f32[512,32,128]{2,1,0:T(8,128)} %bitcast.29), kind=kCustom, calls=%fused_computation.3 | custom fusion | flops 2097152 | bytes 25167872 | tf_op jit(solution)/shard_map/scatter-add | solution.py:19
  498.1 1.2 convert_element_type.33
  499.3 60.2 %reduce-scatter.11.cloned.1.call-done = bf16[8,32,128]{2,1,0:T(8,128)(2,1)} async-done(((bf16[128,32,128]{2,1,0:T(8,128)(2,1)}), bf16[8,32,128]{2,1,0:T(8,128)(2,1)}) %reduce-scatter.11.cloned.1.call-update) | async-done | bytes 65552 | tf_op jit(solution)/shard_map/reduce_scatter | solution.py:41
  (23 shorter events, 1.0 us)
Async XLA Ops:
  7.2 37.4 %all-gather.3.cloned.1.call-start = ((), (), s32[]{:S(2)}) async-start(), calls=%async_computation.4 | async-start | bytes 1114112 | tf_op jit(solution)/shard_map/all_gather | solution.py:34
  7.9 124.0 %reduce-scatter.5.cloned.1.call-start = ((), (), s32[]{:S(2)}) async-start(), calls=%async_computation.5 | async-start | bytes 1179648 | tf_op jit(solution)/shard_map/reduce_scatter | solution.py:36
  49.0 11.0 %copy-start.2 = (s32[64,8]{0,1:T(8,128)S(1)}, s32[64,8]{0,1:T(8,128)}, u32[]{:S(2)}) copy-start(s32[64,8]{0,1:T(8,128)} %param.5) | copy-start | bytes 6148
  59.9 225.6 %reduce-scatter.7.cloned.1.call-start = ((), (), s32[]{:S(2)}) async-start(), calls=%async_computation.6 | async-start | bytes 1114112 | tf_op jit(solution)/shard_map/reduce_scatter | solution.py:41
  132.9 46.2 %copy-start = (bf16[8,32,128]{2,1,0:T(8,128)(2,1)}, bf16[8,32,128]{2,1,0:T(8,128)(2,1)S(1)}, u32[]{:S(2)}) copy-start(bf16[8,32,128]{2,1,0:T(8,128)(2,1)S(1)} %convert_element_type.29) | copy-start | bytes 196612
  225.1 93.4 %all-gather.5.cloned.1.call-start = ((), (), s32[]{:S(2)}) async-start(), calls=%async_computation.7 | async-start | bytes 1114112 | tf_op jit(solution)/shard_map/all_gather | solution.py:34
  285.5 120.5 %reduce-scatter.9.cloned.1.call-start = ((), (), s32[]{:S(2)}) async-start(), calls=%async_computation.8 | async-start | bytes 1179648 | tf_op jit(solution)/shard_map/reduce_scatter | solution.py:36
  333.8 225.7 %reduce-scatter.11.cloned.1.call-start = ((), (), s32[]{:S(2)}) async-start(), calls=%async_computation.9 | async-start | bytes 1114112 | tf_op jit(solution)/shard_map/reduce_scatter | solution.py:41
  406.9 46.4 %copy-start.1 = (bf16[8,32,128]{2,1,0:T(8,128)(2,1)}, bf16[8,32,128]{2,1,0:T(8,128)(2,1)S(1)}, u32[]{:S(2)}) copy-start(bf16[8,32,128]{2,1,0:T(8,128)(2,1)S(1)} %convert_element_type.32) | copy-start | bytes 196612
Sparse Core Ops, SparseCore 0:
  9.7 34.8 all-gather.2
  60.0 71.8 reduce-scatter.4
  225.3 60.1 reduce-scatter.6
  287.6 30.9 all-gather.4
  334.0 71.9 reduce-scatter.8
  499.4 60.0 reduce-scatter.10
where the time goes:
time: 569 us; the launch traced here: 566 us
  waiting for transfers between devices  333 us (59%)
  other arithmetic  94.7 us (17%)
  blocking collectives  70 us (12%)
  matrix products  44.5 us (8%)
  between operations  14.2 us (2%)
  local copies, waits for them, and re-layouts  9.62 us (2%)
    reduce_scatter x2, waiting for transfers between devices, body(): lax.psum_scatter(forward_terms(blocks, picked), 'col', scatter_dimension=...  144 us
    reduce_scatter x2, waiting for transfers between devices, body(): lax.psum_scatter(partial_value.astype(jnp.bfloat16), 'row', scatter_dimen...  120 us
    scatter-add x2, other arithmetic, adjoint_terms(): jax.ops.segment_sum(terms.reshape(slot_total, terms.shape[2], terms.shape...  89.1 us
    all_gather x2, blocking collectives, body(): row_vecs = lax.all_gather(forward_out, 'col', axis=0, tiled=True)  70 us
    all_gather x2, waiting for transfers between devices, body(): column_vecs = lax.all_gather(current, 'row', axis=0, tiled=True)  68.1 us
    dot_general x2, matrix products, adjoint_terms(): jnp.einsum('isrc,ikr->iskc', blocks, row_vecs, preferred_element_type=jnp...  22.7 us
    dot_general x2, matrix products, forward_terms(): jnp.einsum('isrc,iskc->ikr', blocks, picked, preferred_element_type=jnp.f...  21.8 us
  transfers between devices with their start and end apart: 6, of which 6 were waited for; matrix products, arithmetic and copies ran while one was open for 0% of the time, Pallas kernels for 0%

commit v1 on v0

--- a/solution.py
+++ b/solution.py
@@ -36,7 +36,9 @@
         forward_out = lax.psum_scatter(
             forward_terms(blocks, picked), "col", scatter_dimension=0, tiled=True
         ).astype(jnp.bfloat16)
-        row_vecs = lax.all_gather(forward_out, "col", axis=0, tiled=True)
+        row_vecs = jnp.concatenate(
+            lax.all_to_all(jnp.stack([forward_out] * lax.axis_size("col")), "col", 0, 0), axis=0
+        )
         partial_value = adjoint_terms(blocks, columns, active, row_vecs, col_count)
         adjoint_out = lax.psum_scatter(
             partial_value.astype(jnp.bfloat16), "row", scatter_dimension=0, tiled=True

time: 569 us -> 526 us (0.924)
  blocking collectives: 70 us -> 14.5 us
  waiting for transfers between devices: 333 us -> 340 us
    all_gather x2 -> x0, blocking collectives: 70 us -> none  [body(): row_vecs = lax.all_gather(forward_out, 'col', axis=0, tiled=True)]
    all_to_all x0 -> x1, blocking collectives: none -> 14.5 us  [body(): lax.all_to_all(jnp.stack([forward_out] * lax.axis_size('col')), 'col', 0, 0)]
    all_to_all x0 -> x1, waiting for transfers between devices: none -> 9.55 us  [body(): lax.all_to_all(jnp.stack([forward_out] * lax.axis_size('col')), 'col', 0, 0)]
  transfers between devices with their start and end apart: 6 -> 7, of which waited for: 6 -> 7; matrix products, arithmetic and copies ran while one was open for 0% -> 0% of each run, Pallas kernels for 0% -> 0%
where the time goes in v1:
time: 526 us; the launch traced here: 524 us
  waiting for transfers between devices  340 us (65%)
  other arithmetic  94.8 us (18%)
  matrix products  44.5 us (8%)
  blocking collectives  14.5 us (3%)
  between operations  14.2 us (3%)
  local copies, waits for them, and re-layouts  10.6 us (2%)
    reduce_scatter x2, waiting for transfers between devices, body(): lax.psum_scatter(forward_terms(blocks, picked), 'col', scatter_dimension=...  144 us
    reduce_scatter x2, waiting for transfers between devices, body(): lax.psum_scatter(partial_value.astype(jnp.bfloat16), 'row', scatter_dimen...  118 us
    scatter-add x2, other arithmetic, adjoint_terms(): jax.ops.segment_sum(terms.reshape(slot_total, terms.shape[2], terms.shape...  89.1 us
    all_gather x2, waiting for transfers between devices, body(): column_vecs = lax.all_gather(current, 'row', axis=0, tiled=True)  68.3 us
    dot_general x2, matrix products, adjoint_terms(): jnp.einsum('isrc,ikr->iskc', blocks, row_vecs, preferred_element_type=jnp...  22.7 us
    dot_general x2, matrix products, forward_terms(): jnp.einsum('isrc,iskc->ikr', blocks, picked, preferred_element_type=jnp.f...  21.8 us
    all_to_all x1, blocking collectives, body(): lax.all_to_all(jnp.stack([forward_out] * lax.axis_size('col')), 'col', 0, 0)  14.5 us
  transfers between devices with their start and end apart: 7, of which 7 were waited for; matrix products, arithmetic and copies ran while one was open for 0% of the time, Pallas kernels for 0%

profile of v1, /device:TPU:0, one launch (start us, length us, event | category | flops | bytes accessed | tf_op | source)
XLA Modules:
  0.0 523.7 jit_solution(11639336517730831018)
XLA Ops:
  7.9 0.7 compare_select_fusion
  8.8 0.7 fusion.12
  9.6 35.0 %all-gather.3.cloned.1.call-done = bf16[128,32,128]{2,1,0:T(8,128)(2,1)} async-done(((bf16[8,32,128]{2,1,0:T(8,128)(2,1)}), bf16[128,32,128]{2,1,0:T(8,128)(2,1)}) %all-gather.3.cloned.1.call-update) | async-done | bytes 1048592 | tf_op jit(solution)/shard_map/all_gather | solution.py:34
  44.6 4.4 gather_fusion
  49.0 10.9 %fusion.6 = f32[64,32,128]{2,1,0:T(8,128)} fusion(bf16[64,8,128,128]{3,2,1,0:T(8,128)(2,1)} %param.4, bf16[64,8,32,128]{3,2,1,0:T(8,128)(2,1)} %bitcast.34, bf16[64,8]{1,0:T(8,128)(2,1)S(1)} %get-tuple-element.5), kind=kOutput, calls=%fused_computation.12 | convolution fusion | flops 538968064 | bytes 22021120 | tf_op jit(solution)/shard_map/isrc,iskc->ikr/dot_general | solution.py:12
  59.9 72.1 %reduce-scatter.5.cloned.1.call-done = f32[8,32,128]{2,1,0:T(8,128)} async-done(((f32[64,32,128]{2,1,0:T(8,128)}), f32[8,32,128]{2,1,0:T(8,128)}) %reduce-scatter.5.cloned.1.call-update) | async-done | bytes 131088 | tf_op jit(solution)/shard_map/reduce_scatter | solution.py:36
  132.0 0.9 convert_element_type.29
  133.0 0.9 stack.4
  133.8 4.5 all-to-all-start
  138.6 9.6 %all-to-all-done = bf16[8,8,32,128]{3,2,1,0:T(8,128)(2,1)S(1)} async-done(((bf16[8,8,32,128]{3,2,1,0:T(8,128)(2,1)}), bf16[8,8,32,128]{3,2,1,0:T(8,128)(2,1)S(1)}, u32[]{:S(2)}, u32[]{:S(2)}) %all-to-all-start) | async-done | bytes 524320 | tf_op jit(solution)/shard_map/all_to_all | solution.py:40
  148.2 11.3 %broadcast_multiply_fusion.1 = f32[64,32,8,128]{3,1,2,0:T(8,128)} fusion(f32[64,8]{1,0:T(8,128)S(1)} %get-tuple-element.4, bf16[64,32,128,1]{2,1,3,0:T(8,128)(2,1)S(1)} %bitcast.35, bf16[64,8,128,128]{3,2,1,0:T(8,128)(2,1)} %param.4), kind=kOutput, calls=%fused_computation.7 | convolution fusion | flops 538968064 | bytes 25692160 | tf_op jit(solution)/shard_map/isrc,ikr->iskc/dot_general | solution.py:16
  159.7 44.6 %scatter_fusion = f32[128,32,128]{2,1,0:T(8,128)S(1)} fusion(f32[128,32,128]{2,1,0:T(8,128)S(1)} %broadcast.44.clone, s32[512]{0:T(512)S(1)} %reshape.90, f32[512,32,128]{2,1,0:T(8,128)} %bitcast.32), kind=kCustom, calls=%fused_computation.2 | custom fusion | flops 2097152 | bytes 25167872 | tf_op jit(solution)/shard_map/scatter-add | solution.py:19
  204.3 1.2 convert_element_type.31
  205.6 58.9 %reduce-scatter.7.cloned.1.call-done = bf16[8,32,128]{2,1,0:T(8,128)(2,1)} async-done(((bf16[128,32,128]{2,1,0:T(8,128)(2,1)}), bf16[8,32,128]{2,1,0:T(8,128)(2,1)}) %reduce-scatter.7.cloned.1.call-update) | async-done | bytes 65552 | tf_op jit(solution)/shard_map/reduce_scatter | solution.py:43
  264.5 33.3 %all-gather.5.cloned.1.call-done = bf16[128,32,128]{2,1,0:T(8,128)(2,1)} async-done(((bf16[8,32,128]{2,1,0:T(8,128)(2,1)}), bf16[128,32,128]{2,1,0:T(8,128)(2,1)}) %all-gather.5.cloned.1.call-update) | async-done | bytes 1048592 | tf_op jit(solution)/shard_map/all_gather | solution.py:34
  297.8 4.4 gather_fusion.1
  302.2 10.9 %fusion.9 = f32[64,32,128]{2,1,0:T(8,128)} fusion(bf16[64,8,128,128]{3,2,1,0:T(8,128)(2,1)} %param.4, bf16[64,8,32,128]{3,2,1,0:T(8,128)(2,1)} %bitcast.33, bf16[64,8]{1,0:T(8,128)(2,1)S(1)} %get-tuple-element.5), kind=kOutput, calls=%fused_computation.13 | convolution fusion | flops 538968064 | bytes 22021120 | tf_op jit(solution)/shard_map/isrc,iskc->ikr/dot_general | solution.py:12
  313.1 72.1 %reduce-scatter.9.cloned.1.call-done = f32[8,32,128]{2,1,0:T(8,128)} async-done(((f32[64,32,128]{2,1,0:T(8,128)}), f32[8,32,128]{2,1,0:T(8,128)}) %reduce-scatter.9.cloned.1.call-update) | async-done | bytes 131088 | tf_op jit(solution)/shard_map/reduce_scatter | solution.py:36
  385.2 0.9 convert_element_type.32
  386.2 14.5 %all_to_all.10 = bf16[8,8,32,128]{3,2,1,0:T(8,128)(2,1)S(1)} all-to-all(bf16[8,8,32,128]{3,2,1,0:T(8,128)(2,1)S(1)} %stack.5), channel_id=1, replica_groups=mesh['row'=16,'col'=8] {'col'}, dimensions={0} | all-to-all | bytes 1048576 | tf_op jit(solution)/shard_map/all_to_all | solution.py:40
  400.7 11.4 %broadcast_multiply_fusion = f32[64,32,8,128]{3,1,2,0:T(8,128)} fusion(f32[64,8]{1,0:T(8,128)S(1)} %get-tuple-element.4, bf16[64,32,128,1]{2,1,3,0:T(8,128)(2,1)S(1)} %bitcast.36, bf16[64,8,128,128]{3,2,1,0:T(8,128)(2,1)} %param.4), kind=kOutput, calls=%fused_computation.6 | convolution fusion | flops 538968064 | bytes 25692160 | tf_op jit(solution)/shard_map/isrc,ikr->iskc/dot_general | solution.py:16
  412.3 44.6 %scatter_fusion.1 = f32[128,32,128]{2,1,0:T(8,128)S(1)} fusion(f32[128,32,128]{2,1,0:T(8,128)S(1)} %broadcast.44, s32[512]{0:T(512)S(1)} %reshape.90, f32[512,32,128]{2,1,0:T(8,128)} %bitcast.31), kind=kCustom, calls=%fused_computation.3 | custom fusion | flops 2097152 | bytes 25167872 | tf_op jit(solution)/shard_map/scatter-add | solution.py:19
  456.9 1.2 convert_element_type.33
  458.1 58.7 %reduce-scatter.11.cloned.1.call-done = bf16[8,32,128]{2,1,0:T(8,128)(2,1)} async-done(((bf16[128,32,128]{2,1,0:T(8,128)(2,1)}), bf16[8,32,128]{2,1,0:T(8,128)(2,1)}) %reduce-scatter.11.cloned.1.call-update) | async-done | bytes 65552 | tf_op jit(solution)/shard_map/reduce_scatter | solution.py:43
  (26 shorter events, 2.0 us)
Async XLA Ops:
  7.2 37.4 %all-gather.3.cloned.1.call-start = ((), (), s32[]{:S(2)}) async-start(), calls=%async_computation.6 | async-start | bytes 1114112 | tf_op jit(solution)/shard_map/all_gather | solution.py:34
  7.9 124.1 %reduce-scatter.5.cloned.1.call-start = ((), (), s32[]{:S(2)}) async-start(), calls=%async_computation.7 | async-start | bytes 1179648 | tf_op jit(solution)/shard_map/reduce_scatter | solution.py:36
  49.0 89.5 %copy-start.2 = (s32[64,8]{0,1:T(8,128)S(1)}, s32[64,8]{0,1:T(8,128)}, u32[]{:S(2)}) copy-start(s32[64,8]{0,1:T(8,128)} %param.5) | copy-start | bytes 6148
  132.9 26.5 %copy-start = (bf16[8,32,128]{2,1,0:T(8,128)(2,1)}, bf16[8,32,128]{2,1,0:T(8,128)(2,1)S(1)}, u32[]{:S(2)}) copy-start(bf16[8,32,128]{2,1,0:T(8,128)(2,1)S(1)} %convert_element_type.29) | copy-start | bytes 196612
  133.8 14.3 %all-to-all-start = ((bf16[8,8,32,128]{3,2,1,0:T(8,128)(2,1)}), bf16[8,8,32,128]{3,2,1,0:T(8,128)(2,1)S(1)}, u32[]{:S(2)}, u32[]{:S(2)}) async-start(bf16[8,8,32,128]{3,2,1,0:T(8,128)(2,1)} %stack.4), calls=%async_computation.1 | async-start | bytes 1048576 | tf_op jit(solution)/shard_map/all_to_all | solution.py:40
  138.4 126.1 %reduce-scatter.7.cloned.1.call-start = ((), (), s32[]{:S(2)}) async-start(), calls=%async_computation.8 | async-start | bytes 1114112 | tf_op jit(solution)/shard_map/reduce_scatter | solution.py:43
  205.5 92.3 %all-gather.5.cloned.1.call-start = ((), (), s32[]{:S(2)}) async-start(), calls=%async_computation.9 | async-start | bytes 1114112 | tf_op jit(solution)/shard_map/all_gather | solution.py:34
  264.5 120.7 %reduce-scatter.9.cloned.1.call-start = ((), (), s32[]{:S(2)}) async-start(), calls=%async_computation.10 | async-start | bytes 1179648 | tf_op jit(solution)/shard_map/reduce_scatter | solution.py:36
  313.1 203.7 %reduce-scatter.11.cloned.1.call-start = ((), (), s32[]{:S(2)}) async-start(), calls=%async_computation.11 | async-start | bytes 1114112 | tf_op jit(solution)/shard_map/reduce_scatter | solution.py:43
  386.1 25.9 %copy-start.1 = (bf16[8,32,128]{2,1,0:T(8,128)(2,1)}, bf16[8,32,128]{2,1,0:T(8,128)(2,1)S(1)}, u32[]{:S(2)}) copy-start(bf16[8,32,128]{2,1,0:T(8,128)(2,1)S(1)} %convert_element_type.32) | copy-start | bytes 196612
Sparse Core Ops, SparseCore 0:
  9.7 34.8 all-gather.2
  60.0 71.9 reduce-scatter.4
  205.6 58.7 reduce-scatter.6
  266.6 31.1 all-gather.4
  313.2 71.9 reduce-scatter.8
  458.2 58.5 reduce-scatter.10
